TPU v7x, 32 devices: a whole 2x2x4 slice. The times are simulated.
32 devices in a mesh: row: 4 (over y, x), col: 8 (over z, core).
Axes of the slice: x: 2, y: 2, z: 4, core: 2. Of those that a mesh axis runs over, the one named last changes fastest.
Arguments:
- normals: float32 [2048, 16384], P('row', 'col'), may hold values from -6 to 6
- factor: float32 [16384, 16384], P('row', 'col'), as said below
- cell_entity: int32 [16384], P('row'), may hold values from 0 to 1023
- scale: float32 [16384], P('row'), may hold values from 0.25 to 2
- volatility: float32 [16384], P('row'), may hold values from 0.1 to 0.6
- retention: int32 [16384], P('row'), may hold values from 1 to 11
- limit: int32 [16384], P('row'), may hold values from 1 to 15
Outputs:
- entity_loss: float32 [2, 2048, 1024], P(None, 'col', 'row')
Inputs may be any that keep to these rules, and one draw needn't show every extreme that they name: factor is zero above the diagonal and one on it.
All inputs are finite; a program needn't handle non-finite values.
Results may differ from a plain program's by a relative error of at most 0.000078.
Values sent between devices are 32-bit elements; how exact they have to be, the bound alone decides.
A program may use at most 128 MiB of HBM per device.

v0:
```python
import jax
import jax.numpy as jnp
from jax import lax
from jax.sharding import PartitionSpec as P

ENT = 1024


def body(normals, factor, cell_entity, scale, volatility, retention, limit):
    partial_sum = lax.dot_general(
        lax.all_gather(normals, "row", axis=0, tiled=True),
        factor,
        (((1,), (1,)), ((), ())),
        precision=lax.Precision.HIGHEST,
        preferred_element_type=jnp.float32,
    )
    norms = lax.psum(jnp.sum(factor * factor, axis=1), "col")
    mixed = lax.psum_scatter(partial_sum, "col", scatter_dimension=0, tiled=True)
    cell_norms, cell_scale, cell_vol = (norms, scale, volatility)
    cell_ret, cell_lim, cell_ent = (retention, limit, cell_entity)
    correlated = mixed * lax.rsqrt(cell_norms)[None, :]
    ground = cell_scale[None, :] * jnp.exp(cell_vol[None, :] * correlated)
    floor_level = 0.25 * cell_ret.astype(jnp.float32)
    cover = 0.25 * cell_lim.astype(jnp.float32)
    ceded = jnp.minimum(jnp.maximum(ground - floor_level[None, :], 0.0), cover[None, :])
    net = ground - ceded
    onehot = (cell_ent[:, None] == jnp.arange(ENT, dtype=jnp.int32)[None, :]).astype(jnp.float32)
    stacked = jnp.stack([net, ceded])
    local_sums = jnp.einsum("ksc,ce->kse", stacked, onehot, precision=lax.Precision.HIGHEST)
    return lax.psum_scatter(local_sums, "row", scatter_dimension=2, tiled=True)


def solution(mesh):
    return jax.shard_map(
        body,
        mesh=mesh,
        in_specs=(
            P("row", "col"),
            P("row", "col"),
            P("row"),
            P("row"),
            P("row"),
            P("row"),
            P("row"),
        ),
        out_specs=P(None, "col", "row"),
        check_vma=False,
    )
```

profile of v0, /device:TPU:0, one launch (start us, length us, event | category | flops | bytes accessed | tf_op | source)
XLA Modules:
  0.0 780.9 jit_solution(6835023982449881091)
XLA Ops:
  6.5 0.0 all-gather.2.cloned.1.call-start
  6.5 0.7 all-gather.2.cloned.1.call-update
  7.3 0.0 reduce-scatter.3.cloned.1.call-start
  7.3 162.0 %all-gather.2.cloned.1.call-done = f32[2048,2048]{1,0:T(8,128)} async-done(((f32[512,2048]{1,0:T(8,128)}), f32[2048,2048]{1,0:T(8,128)}) %all-gather.2.cloned.1.call-update) | async-done | bytes 16777232 | tf_op jit(solution)/shard_map/all_gather | solution.py:11
  169.3 225.8 %fusion.9 = f32[2048,4096]{1,0:T(8,128)} fusion(f32[2048,2048]{1,0:T(8,128)} %all-gather.2.cloned.1.call-done, f32[4096,2048]{1,0:T(8,128)} %param.8), kind=kOutput, calls=%fused_computation.15 | convolution fusion | flops 206158430208 | bytes 83886080 | tf_op jit(solution)/shard_map/dot_general | solution.py:10
  395.1 0.0 reduce-scatter.3.cloned.1.call-update
  395.1 0.0 copy-start.2
  395.1 0.0 copy-start.3
  395.2 0.0 copy-start
  395.2 0.0 copy-start.1
  395.2 0.0 reduce-scatter.5.cloned.1.call-start
  395.2 12.6 %multiply_reduce_fusion = f32[4096]{0:T(1024)S(1)} fusion(f32[4096,2048]{1,0:T(8,128)} %param.8), kind=kLoop, calls=%fused_computation | loop fusion | flops 16773120 | bytes 33570816 | tf_op jit(solution)/shard_map/reduce_sum | solution.py:17
  407.8 30.9 %psum.7 = f32[4096]{0:T(1024)S(1)} all-reduce(f32[4096]{0:T(1024)S(1)} %multiply_reduce_fusion), channel_id=1, replica_groups=mesh['row'=4,'col'=8] {'col'}, use_global_device_ids=true, to_apply=%region_2.0 | all-reduce | flops 4096 | bytes 32768 | tf_op jit(solution)/shard_map/psum | solution.py:17
  438.7 0.0 copy-done.2
  438.7 0.0 copy-done.3
  438.7 282.7 %reduce-scatter.3.cloned.1.call-done = f32[256,4096]{1,0:T(8,128)} async-done(((f32[2048,4096]{1,0:T(8,128)}), f32[256,4096]{1,0:T(8,128)}) %reduce-scatter.3.cloned.1.call-update) | async-done | bytes 4194320 | tf_op jit(solution)/shard_map/reduce_scatter | solution.py:18
  721.4 0.0 copy-done
  721.4 0.0 copy-done.1
  721.4 0.0 copy-start.4
  721.4 3.8 subtract_bitcast_fusion
  725.2 0.0 copy-done.4
  725.2 15.4 %fusion.1 = f32[2,256,1024]{2,1,0:T(8,128)} fusion(f32[1,256,4096]{2,1,0:T(8,128)S(1)} %get-tuple-element.6, f32[1,256,4096]{2,1,0:T(8,128)S(1)} %get-tuple-element.5, s32[4096]{0:T(1024)S(1)} %copy-done.4), kind=kOutput, calls=%fused_computation.3 | convolution fusion | flops 25776095232 | bytes 10502144 | tf_op jit(solution)/shard_map/ksc,ce->kse/dot_general | solution.py:29
  740.6 0.0 reduce-scatter.5.cloned.1.call-update
  740.6 33.7 %reduce-scatter.5.cloned.1.call-done = f32[2,256,256]{2,1,0:T(8,128)} async-done(((f32[2,256,1024]{2,1,0:T(8,128)}), f32[2,256,256]{2,1,0:T(8,128)}) %reduce-scatter.5.cloned.1.call-update) | async-done | bytes 524304 | tf_op jit(solution)/shard_map/reduce_scatter | solution.py:30
  (2 shorter events, 0.0 us)
Async XLA Ops:
  6.5 162.8 %all-gather.2.cloned.1.call-start = ((), (), s32[]{:S(2)}) async-start(), calls=%async_computation.2 | async-start | bytes 20971520 | tf_op jit(solution)/shard_map/all_gather | solution.py:11
  7.3 714.2 %reduce-scatter.3.cloned.1.call-start = ((), (), s32[]{:S(2)}) async-start(), calls=%async_computation.3 | async-start | bytes 37748736 | tf_op jit(solution)/shard_map/reduce_scatter | solution.py:18
  395.1 43.6 %copy-start.2 = (s32[4096]{0:T(1024)S(1)}, s32[4096]{0:T(1024)}, u32[]{:S(2)}) copy-start(s32[4096]{0:T(1024)} %param.13) | copy-start | bytes 49156
  395.1 43.6 %copy-start.3 = (s32[4096]{0:T(1024)S(1)}, s32[4096]{0:T(1024)}, u32[]{:S(2)}) copy-start(s32[4096]{0:T(1024)} %param.12) | copy-start | bytes 49156
  395.2 326.3 %copy-start = (f32[4096]{0:T(1024)S(1)}, f32[4096]{0:T(1024)}, u32[]{:S(2)}) copy-start(f32[4096]{0:T(1024)} %param.11) | copy-start | bytes 49156
  395.2 326.3 %copy-start.1 = (f32[4096]{0:T(1024)S(1)}, f32[4096]{0:T(1024)}, u32[]{:S(2)}) copy-start(f32[4096]{0:T(1024)} %param.10) | copy-start | bytes 49156
  395.2 379.1 %reduce-scatter.5.cloned.1.call-start = ((), (), s32[]{:S(2)}) async-start(), calls=%async_computation.4 | async-start | bytes 2621440 | tf_op jit(solution)/shard_map/reduce_scatter | solution.py:30
  721.4 3.8 copy-start.4
Sparse Core Ops, SparseCore 0:
  9.2 160.1 all-gather.1
  395.3 326.1 reduce-scatter.2
  740.7 33.5 reduce-scatter.4
where the time goes:
time: 781 us
  waiting for transfers between devices  479 us (61%)
  matrix products  241 us (31%)
  blocking collectives  30.9 us (4%)
  other arithmetic  16.4 us (2%)
  between operations  13.2 us (2%)
    reduce_scatter x1, waiting for transfers between devices, body(): lax.psum_scatter(partial_sum, 'col', scatter_dimension=0, tiled=True)  283 us
    dot_general x1, matrix products, body(): lax.dot_general(lax.all_gather(normals, 'row', axis=0, tiled=True), facto...  226 us
    all_gather x1, waiting for transfers between devices, body(): lax.all_gather(normals, 'row', axis=0, tiled=True)  162 us
    reduce_scatter x1, waiting for transfers between devices, body(): return lax.psum_scatter(local_sums, 'row', scatter_dimension=2, tiled=True)  33.7 us
    psum x1, blocking collectives, body(): norms = lax.psum(jnp.sum(factor * factor, axis=1), 'col')  30.9 us
  transfers between devices with their start and end apart: 3, of which 3 were waited for; matrix products, arithmetic and copies ran while one was open for 2% of the time, Pallas kernels for 0%

commit v1 on v0

v1 whole, which is shorter than its diff:
```python
import jax
import jax.numpy as jnp
from jax import lax
from jax.sharding import PartitionSpec as P

ENT = 1024
CHUNKS = 4


def body(normals, factor, cell_entity, scale, volatility, retention, limit):
    rows, cols = lax.axis_size("row"), lax.axis_size("col")
    scen, depth = normals.shape
    per_col = scen * rows // cols
    step = per_col // CHUNKS
    blocks = normals.reshape(scen // per_col, CHUNKS, step, depth)
    norms = lax.psum(jnp.sum(factor * factor, axis=1), "col")
    floor_level = 0.25 * retention.astype(jnp.float32)
    cover = 0.25 * limit.astype(jnp.float32)
    gain = volatility * lax.rsqrt(norms)
    onehot = (cell_entity[:, None] == jnp.arange(ENT, dtype=jnp.int32)[None, :]).astype(jnp.float32)
    mixed = []
    for k in range(CHUNKS):
        gathered = lax.all_gather(blocks[:, k].reshape(-1, depth), "row", axis=0, tiled=True)
        partial_sum = lax.dot_general(
            gathered,
            factor,
            (((1,), (1,)), ((), ())),
            precision=lax.Precision.HIGH,
            preferred_element_type=jnp.float32,
        )
        mixed.append(lax.psum_scatter(partial_sum, "col", scatter_dimension=0, tiled=True))
    sums = []
    for part in mixed:
        ground = scale[None, :] * jnp.exp(gain[None, :] * part)
        ceded = jnp.minimum(jnp.maximum(ground - floor_level[None, :], 0.0), cover[None, :])
        net = ground - ceded
        stacked = jnp.stack([net, ceded])
        sums.append(jnp.einsum("ksc,ce->kse", stacked, onehot, precision=lax.Precision.HIGH))
    local_sums = jnp.concatenate(sums, axis=1)
    return lax.psum_scatter(local_sums, "row", scatter_dimension=2, tiled=True)


def solution(mesh):
    return jax.shard_map(
        body,
        mesh=mesh,
        in_specs=(
            P("row", "col"),
            P("row", "col"),
            P("row"),
            P("row"),
            P("row"),
            P("row"),
            P("row"),
        ),
        out_specs=P(None, "col", "row"),
        check_vma=False,
    )
```

time: 781 us -> 664 us (0.85)
  matrix products: 241 us -> 151 us
  waiting for transfers between devices: 479 us -> 439 us
    dot_general x2 -> x8, matrix products: 241 us -> 151 us  [the longest x4 133 us: body(): lax.dot_general(gathered, factor, (((1,), (1,)), ((), ())), precision=lax...]
    all_gather x1 -> x4, waiting for transfers between devices: 162 us -> 117 us  [body(): lax.all_gather(blocks[:, k].reshape(-1, depth), 'row', axis=0, tiled=True)]
    reduce_scatter x1 -> x4, waiting for transfers between devices: 283 us -> 287 us  [body(): lax.psum_scatter(partial_sum, 'col', scatter_dimension=0, tiled=True)]
  transfers between devices with their start and end apart: 3 -> 9, of which waited for: 3 -> 9; matrix products, arithmetic and copies ran while one was open for 2% -> 22% of each run, Pallas kernels for 0% -> 0%
where the time goes in v1:
time: 664 us; the launch traced here: 658 us
  waiting for transfers between devices  439 us (66%)
  matrix products  151 us (23%)
  blocking collectives  30.6 us (5%)
  other arithmetic  17.7 us (3%)
  between operations  13.6 us (2%)
    reduce_scatter x4, waiting for transfers between devices, body(): lax.psum_scatter(partial_sum, 'col', scatter_dimension=0, tiled=True)  287 us
    dot_general x4, matrix products, body(): lax.dot_general(gathered, factor, (((1,), (1,)), ((), ())), precision=lax...  133 us
    all_gather x4, waiting for transfers between devices, body(): lax.all_gather(blocks[:, k].reshape(-1, depth), 'row', axis=0, tiled=True)  117 us
    reduce_scatter x1, waiting for transfers between devices, body(): return lax.psum_scatter(local_sums, 'row', scatter_dimension=2, tiled=True)  33.7 us
    psum x1, blocking collectives, body(): norms = lax.psum(jnp.sum(factor * factor, axis=1), 'col')  30.6 us
    dot_general x4, matrix products, body(): jnp.einsum('ksc,ce->kse', stacked, onehot, precision=lax.Precision.HIGH)  18.6 us
  transfers between devices with their start and end apart: 9, of which 9 were waited for; matrix products, arithmetic and copies ran while one was open for 22% of the time, Pallas kernels for 0%

profile of v1, /device:TPU:0, one launch (start us, length us, event | category | flops | bytes accessed | tf_op | source)
XLA Modules:
  0.0 657.5 jit_solution(5651818274367085392)
XLA Ops:
  6.5 0.0 all-gather.9.cloned.1.call-start
  6.5 4.3 fusion.33
  10.8 0.0 all-gather.9.cloned.1.call-update
  10.9 0.0 all-gather.11.cloned.1.call-start
  10.9 0.7 all-gather.11.cloned.1.call-update
  11.6 0.0 all-gather.5.cloned.1.call-start
  11.7 0.7 all-gather.5.cloned.1.call-update
  12.3 0.0 all-gather.7.cloned.1.call-start
  12.4 0.5 all-gather.7.cloned.1.call-update
  12.9 0.0 reduce-scatter.10.cloned.1.call-start
  13.0 53.4 %all-gather.9.cloned.1.call-done = f32[512,2048]{1,0:T(8,128)} async-done(((f32[128,2048]{1,0:T(8,128)}), f32[512,2048]{1,0:T(8,128)}) %all-gather.9.cloned.1.call-update) | async-done | bytes 4194320 | tf_op jit(solution)/shard_map/all_gather | solution.py:23
  66.4 33.1 %fusion.36 = f32[512,4096]{1,0:T(8,128)} fusion(f32[512,2048]{1,0:T(8,128)} %all-gather.9.cloned.1.call-done, f32[4096,2048]{1,0:T(8,128)} %param.8), kind=kOutput, calls=%fused_computation.50 | convolution fusion | flops 25769803776 | bytes 46137344 | tf_op jit(solution)/shard_map/dot_general | solution.py:24
  99.5 0.0 reduce-scatter.10.cloned.1.call-update
  99.6 0.3 reduce-scatter.12.cloned.1.call-start
  99.8 21.2 %all-gather.11.cloned.1.call-done = f32[512,2048]{1,0:T(8,128)} async-done(((f32[128,2048]{1,0:T(8,128)}), f32[512,2048]{1,0:T(8,128)}) %all-gather.11.cloned.1.call-update) | async-done | bytes 4194320 | tf_op jit(solution)/shard_map/all_gather | solution.py:23
  121.0 33.1 %fusion.37 = f32[512,4096]{1,0:T(8,128)} fusion(f32[512,2048]{1,0:T(8,128)} %all-gather.11.cloned.1.call-done, f32[4096,2048]{1,0:T(8,128)} %param.8), kind=kOutput, calls=%fused_computation.51 | convolution fusion | flops 25769803776 | bytes 46137344 | tf_op jit(solution)/shard_map/dot_general | solution.py:24
  154.1 0.0 reduce-scatter.12.cloned.1.call-update
  154.1 0.3 reduce-scatter.6.cloned.1.call-start
  154.4 21.2 %all-gather.5.cloned.1.call-done = f32[512,2048]{1,0:T(8,128)} async-done(((f32[128,2048]{1,0:T(8,128)}), f32[512,2048]{1,0:T(8,128)}) %all-gather.5.cloned.1.call-update) | async-done | bytes 4194320 | tf_op jit(solution)/shard_map/all_gather | solution.py:23
  175.6 33.1 %fusion.34 = f32[512,4096]{1,0:T(8,128)} fusion(f32[512,2048]{1,0:T(8,128)} %all-gather.5.cloned.1.call-done, f32[4096,2048]{1,0:T(8,128)} %param.8), kind=kOutput, calls=%fused_computation.48 | convolution fusion | flops 25769803776 | bytes 46137344 | tf_op jit(solution)/shard_map/dot_general | solution.py:24
  208.7 0.0 reduce-scatter.6.cloned.1.call-update
  208.8 0.5 reduce-scatter.8.cloned.1.call-start
  209.3 20.8 %all-gather.7.cloned.1.call-done = f32[512,2048]{1,0:T(8,128)} async-done(((f32[128,2048]{1,0:T(8,128)}), f32[512,2048]{1,0:T(8,128)}) %all-gather.7.cloned.1.call-update) | async-done | bytes 4194320 | tf_op jit(solution)/shard_map/all_gather | solution.py:23
  230.0 33.1 %fusion.35 = f32[512,4096]{1,0:T(8,128)} fusion(f32[512,2048]{1,0:T(8,128)} %all-gather.7.cloned.1.call-done, f32[4096,2048]{1,0:T(8,128)} %param.8), kind=kOutput, calls=%fused_computation.49 | convolution fusion | flops 25769803776 | bytes 46137344 | tf_op jit(solution)/shard_map/dot_general | solution.py:24
  263.1 0.0 reduce-scatter.8.cloned.1.call-update
  263.1 0.0 copy-start.1
  263.2 0.0 copy-start.2
  263.2 0.0 copy-start.3
  263.2 0.0 copy-start
  263.2 0.0 reduce-scatter.14.cloned.1.call-start
  263.2 12.5 %multiply_reduce_fusion = f32[4096]{0:T(1024)S(1)} fusion(f32[4096,2048]{1,0:T(8,128)} %param.8), kind=kLoop, calls=%fused_computation | loop fusion | flops 16773120 | bytes 33570816 | tf_op jit(solution)/shard_map/reduce_sum | solution.py:16
  275.7 30.6 %psum.7 = f32[4096]{0:T(1024)S(1)} all-reduce(f32[4096]{0:T(1024)S(1)} %multiply_reduce_fusion), channel_id=1, replica_groups=mesh['row'=4,'col'=8] {'col'}, use_global_device_ids=true, to_apply=%region_1.0 | all-reduce | flops 4096 | bytes 32768 | tf_op jit(solution)/shard_map/psum | solution.py:16
  306.4 0.0 copy-done.1
  306.4 0.0 copy-done.2
  306.4 0.0 copy-done.3
  306.4 16.0 %reduce-scatter.10.cloned.1.call-done = f32[64,4096]{1,0:T(8,128)} async-done(((f32[512,4096]{1,0:T(8,128)}), f32[64,4096]{1,0:T(8,128)}) %reduce-scatter.10.cloned.1.call-update) | async-done | bytes 1048592 | tf_op jit(solution)/shard_map/reduce_scatter | solution.py:31
  322.4 90.1 %reduce-scatter.12.cloned.1.call-done = f32[64,4096]{1,0:T(8,128)} async-done(((f32[512,4096]{1,0:T(8,128)}), f32[64,4096]{1,0:T(8,128)}) %reduce-scatter.12.cloned.1.call-update) | async-done | bytes 1048592 | tf_op jit(solution)/shard_map/reduce_scatter | solution.py:31
  412.6 90.3 %reduce-scatter.6.cloned.1.call-done = f32[64,4096]{1,0:T(8,128)} async-done(((f32[512,4096]{1,0:T(8,128)}), f32[64,4096]{1,0:T(8,128)}) %reduce-scatter.6.cloned.1.call-update) | async-done | bytes 1048592 | tf_op jit(solution)/shard_map/reduce_scatter | solution.py:31
  502.8 90.3 %reduce-scatter.8.cloned.1.call-done = f32[64,4096]{1,0:T(8,128)} async-done(((f32[512,4096]{1,0:T(8,128)}), f32[64,4096]{1,0:T(8,128)}) %reduce-scatter.8.cloned.1.call-update) | async-done | bytes 1048592 | tf_op jit(solution)/shard_map/reduce_scatter | solution.py:31
  593.1 0.0 copy-done
  593.1 0.0 copy-start.4
  593.1 3.8 subtract_bitcast_fusion.3
  596.9 0.0 copy-done.4
  596.9 4.6 fusion.7
  601.5 4.6 fusion.5
  606.1 4.8 fusion.3
  611.0 4.6 fusion.1
  615.6 1.5 pad_maximum_fusion
  617.0 0.0 reduce-scatter.14.cloned.1.call-update
  617.1 33.7 %reduce-scatter.14.cloned.1.call-done = f32[2,256,256]{2,1,0:T(8,128)} async-done(((f32[2,256,1024]{2,1,0:T(8,128)}), f32[2,256,256]{2,1,0:T(8,128)}) %reduce-scatter.14.cloned.1.call-update) | async-done | bytes 524304 | tf_op jit(solution)/shard_map/reduce_scatter | solution.py:40
  (2 shorter events, 0.0 us)
Async XLA Ops:
  6.5 59.9 %all-gather.9.cloned.1.call-start = ((), (), s32[]{:S(2)}) async-start(), calls=%async_computation.9 | async-start | bytes 5242880 | tf_op jit(solution)/shard_map/all_gather | solution.py:23
  10.9 110.1 %all-gather.11.cloned.1.call-start = ((), (), s32[]{:S(2)}) async-start(), calls=%async_computation.11 | async-start | bytes 5242880 | tf_op jit(solution)/shard_map/all_gather | solution.py:23
  11.6 164.0 %all-gather.5.cloned.1.call-start = ((), (), s32[]{:S(2)}) async-start(), calls=%async_computation.5 | async-start | bytes 5242880 | tf_op jit(solution)/shard_map/all_gather | solution.py:23
  12.3 217.7 %all-gather.7.cloned.1.call-start = ((), (), s32[]{:S(2)}) async-start(), calls=%async_computation.7 | async-start | bytes 5242880 | tf_op jit(solution)/shard_map/all_gather | solution.py:23
  12.9 309.5 %reduce-scatter.10.cloned.1.call-start = ((), (), s32[]{:S(2)}) async-start(), calls=%async_computation.10 | async-start | bytes 9437184 | tf_op jit(solution)/shard_map/reduce_scatter | solution.py:31
  99.6 313.0 %reduce-scatter.12.cloned.1.call-start = ((), (), s32[]{:S(2)}) async-start(), calls=%async_computation.12 | async-start | bytes 9437184 | tf_op jit(solution)/shard_map/reduce_scatter | solution.py:31
  154.1 348.7 %reduce-scatter.6.cloned.1.call-start = ((), (), s32[]{:S(2)}) async-start(), calls=%async_computation.6 | async-start | bytes 9437184 | tf_op jit(solution)/shard_map/reduce_scatter | solution.py:31
  208.8 384.4 %reduce-scatter.8.cloned.1.call-start = ((), (), s32[]{:S(2)}) async-start(), calls=%async_computation.8 | async-start | bytes 9437184 | tf_op jit(solution)/shard_map/reduce_scatter | solution.py:31
  263.1 43.2 %copy-start.1 = (f32[4096]{0:T(1024)S(1)}, f32[4096]{0:T(1024)}, u32[]{:S(2)}) copy-start(f32[4096]{0:T(1024)} %param.11) | copy-start | bytes 49156
  263.2 43.2 %copy-start.2 = (s32[4096]{0:T(1024)S(1)}, s32[4096]{0:T(1024)}, u32[]{:S(2)}) copy-start(s32[4096]{0:T(1024)} %param.13) | copy-start | bytes 49156
  263.2 43.2 %copy-start.3 = (s32[4096]{0:T(1024)S(1)}, s32[4096]{0:T(1024)}, u32[]{:S(2)}) copy-start(s32[4096]{0:T(1024)} %param.12) | copy-start | bytes 49156
  263.2 329.9 %copy-start = (f32[4096]{0:T(1024)S(1)}, f32[4096]{0:T(1024)}, u32[]{:S(2)}) copy-start(f32[4096]{0:T(1024)} %param.10) | copy-start | bytes 49156
  263.2 387.6 %reduce-scatter.14.cloned.1.call-start = ((), (), s32[]{:S(2)}) async-start(), calls=%async_computation.13 | async-start | bytes 2621440 | tf_op jit(solution)/shard_map/reduce_scatter | solution.py:40
  593.1 3.8 copy-start.4
Sparse Core Ops, SparseCore 0:
  11.0 55.3 all-gather.8
  68.3 52.6 all-gather.10
  122.8 52.6 all-gather.4
  177.3 52.6 all-gather.6
  232.2 90.2 reduce-scatter.9
  324.6 87.9 reduce-scatter.11
  414.8 87.9 reduce-scatter.5
  505.1 87.9 reduce-scatter.7
  617.2 33.5 reduce-scatter.13

commit v2 on v1

--- a/solution.py
+++ b/solution.py
@@ -4,7 +4,7 @@
 from jax.sharding import PartitionSpec as P
 
 ENT = 1024
-CHUNKS = 4
+CHUNKS = 2
 
 
 def body(normals, factor, cell_entity, scale, volatility, retention, limit):

time: 664 us -> 599 us (0.902)
  waiting for transfers between devices: 439 us -> 389 us
  matrix products: 151 us -> 134 us
    reduce_scatter x4 -> x2, waiting for transfers between devices: 287 us -> 236 us  [body(): lax.psum_scatter(partial_sum, 'col', scatter_dimension=0, tiled=True)]
    dot_general x4 -> x2, matrix products: 133 us -> 122 us  [body(): lax.dot_general(gathered, factor, (((1,), (1,)), ((), ())), precision=lax...]
    dot_general x4 -> x2, matrix products: 18.6 us -> 11.6 us  [body(): jnp.einsum('ksc,ce->kse', stacked, onehot, precision=lax.Precision.HIGH)]
    all_gather x4 -> x2, waiting for transfers between devices: 117 us -> 118 us  [body(): lax.all_gather(blocks[:, k].reshape(-1, depth), 'row', axis=0, tiled=True)]
  transfers between devices with their start and end apart: 9 -> 5, of which waited for: 9 -> 5; matrix products, arithmetic and copies ran while one was open for 22% -> 23% of each run, Pallas kernels for 0% -> 0%
where the time goes in v2:
time: 599 us; the launch traced here: 589 us
  waiting for transfers between devices  389 us (65%)
  matrix products  134 us (22%)
  blocking collectives  29.9 us (5%)
  other arithmetic  17.6 us (3%)
  between operations  13.4 us (2%)
    reduce_scatter x2, waiting for transfers between devices, body(): lax.psum_scatter(partial_sum, 'col', scatter_dimension=0, tiled=True)  236 us
    dot_general x2, matrix products, body(): lax.dot_general(gathered, factor, (((1,), (1,)), ((), ())), precision=lax...  122 us
    all_gather x2, waiting for transfers between devices, body(): lax.all_gather(blocks[:, k].reshape(-1, depth), 'row', axis=0, tiled=True)  118 us
    reduce_scatter x1, waiting for transfers between devices, body(): return lax.psum_scatter(local_sums, 'row', scatter_dimension=2, tiled=True)  33.7 us
    psum x1, blocking collectives, body(): norms = lax.psum(jnp.sum(factor * factor, axis=1), 'col')  29.9 us
    reduce_sum x1, other arithmetic, body(): norms = lax.psum(jnp.sum(factor * factor, axis=1), 'col')  12.4 us
  transfers between devices with their start and end apart: 5, of which 5 were waited for; matrix products, arithmetic and copies ran while one was open for 23% of the time, Pallas kernels for 0%

profile of v2, /device:TPU:0, one launch (start us, length us, event | category | flops | bytes accessed | tf_op | source)
XLA Modules:
  0.0 588.5 jit_solution(8194489140208767764)
XLA Ops:
  6.5 0.0 all-gather.3.cloned.1.call-start
  6.5 4.7 fusion.17
  11.2 0.0 all-gather.3.cloned.1.call-update
  11.3 0.0 all-gather.5.cloned.1.call-start
  11.3 0.7 all-gather.5.cloned.1.call-update
  12.0 0.0 reduce-scatter.4.cloned.1.call-start
  12.1 89.7 %all-gather.3.cloned.1.call-done = f32[1024,2048]{1,0:T(8,128)} async-done(((f32[256,2048]{1,0:T(8,128)}), f32[1024,2048]{1,0:T(8,128)}) %all-gather.3.cloned.1.call-update) | async-done | bytes 8388624 | tf_op jit(solution)/shard_map/all_gather | solution.py:23
  101.7 60.7 %fusion.18 = f32[1024,4096]{1,0:T(8,128)} fusion(f32[1024,2048]{1,0:T(8,128)} %all-gather.3.cloned.1.call-done, f32[4096,2048]{1,0:T(8,128)} %param.8), kind=kOutput, calls=%fused_computation.28 | convolution fusion | flops 51539607552 | bytes 58720256 | tf_op jit(solution)/shard_map/dot_general | solution.py:24
  162.4 0.0 reduce-scatter.4.cloned.1.call-update
  162.5 0.0 reduce-scatter.6.cloned.1.call-start
  162.5 28.7 %all-gather.5.cloned.1.call-done = f32[1024,2048]{1,0:T(8,128)} async-done(((f32[256,2048]{1,0:T(8,128)}), f32[1024,2048]{1,0:T(8,128)}) %all-gather.5.cloned.1.call-update) | async-done | bytes 8388624 | tf_op jit(solution)/shard_map/all_gather | solution.py:23
  191.2 61.2 %fusion.19 = f32[1024,4096]{1,0:T(8,128)} fusion(f32[1024,2048]{1,0:T(8,128)} %all-gather.5.cloned.1.call-done, f32[4096,2048]{1,0:T(8,128)} %param.8), kind=kOutput, calls=%fused_computation.29 | convolution fusion | flops 51539607552 | bytes 58720256 | tf_op jit(solution)/shard_map/dot_general | solution.py:24
  252.5 0.0 reduce-scatter.6.cloned.1.call-update
  252.5 0.0 copy-start.1
  252.5 0.0 copy-start.2
  252.5 0.0 copy-start.3
  252.5 0.0 copy-start
  252.5 0.0 reduce-scatter.8.cloned.1.call-start
  252.6 12.4 %multiply_reduce_fusion = f32[4096]{0:T(1024)S(1)} fusion(f32[4096,2048]{1,0:T(8,128)} %param.8), kind=kLoop, calls=%fused_computation | loop fusion | flops 16773120 | bytes 33570816 | tf_op jit(solution)/shard_map/reduce_sum | solution.py:16
  265.0 29.9 %psum.7 = f32[4096]{0:T(1024)S(1)} all-reduce(f32[4096]{0:T(1024)S(1)} %multiply_reduce_fusion), channel_id=1, replica_groups=mesh['row'=4,'col'=8] {'col'}, use_global_device_ids=true, to_apply=%region_1.0 | all-reduce | flops 4096 | bytes 32768 | tf_op jit(solution)/shard_map/psum | solution.py:16
  295.0 0.0 copy-done.1
  295.0 0.0 copy-done.2
  295.0 0.0 copy-done.3
  295.0 67.5 %reduce-scatter.4.cloned.1.call-done = f32[128,4096]{1,0:T(8,128)} async-done(((f32[1024,4096]{1,0:T(8,128)}), f32[128,4096]{1,0:T(8,128)}) %reduce-scatter.4.cloned.1.call-update) | async-done | bytes 2097168 | tf_op jit(solution)/shard_map/reduce_scatter | solution.py:31
  362.5 168.9 %reduce-scatter.6.cloned.1.call-done = f32[128,4096]{1,0:T(8,128)} async-done(((f32[1024,4096]{1,0:T(8,128)}), f32[128,4096]{1,0:T(8,128)}) %reduce-scatter.6.cloned.1.call-update) | async-done | bytes 2097168 | tf_op jit(solution)/shard_map/reduce_scatter | solution.py:31
  531.3 0.0 copy-done
  531.3 0.0 copy-start.4
  531.3 3.6 subtract_bitcast_fusion.1
  535.0 0.0 copy-done.4
  535.0 5.8 fusion.3
  540.8 5.8 fusion.1
  546.6 1.5 pad_maximum_fusion
  548.1 0.0 reduce-scatter.8.cloned.1.call-update
  548.1 33.7 %reduce-scatter.8.cloned.1.call-done = f32[2,256,256]{2,1,0:T(8,128)} async-done(((f32[2,256,1024]{2,1,0:T(8,128)}), f32[2,256,256]{2,1,0:T(8,128)}) %reduce-scatter.8.cloned.1.call-update) | async-done | bytes 524304 | tf_op jit(solution)/shard_map/reduce_scatter | solution.py:40
  (2 shorter events, 0.0 us)
Async XLA Ops:
  6.5 95.2 %all-gather.3.cloned.1.call-start = ((), (), s32[]{:S(2)}) async-start(), calls=%async_computation.3 | async-start | bytes 10485760 | tf_op jit(solution)/shard_map/all_gather | solution.py:23
  11.3 180.0 %all-gather.5.cloned.1.call-start = ((), (), s32[]{:S(2)}) async-start(), calls=%async_computation.5 | async-start | bytes 10485760 | tf_op jit(solution)/shard_map/all_gather | solution.py:23
  12.0 350.5 %reduce-scatter.4.cloned.1.call-start = ((), (), s32[]{:S(2)}) async-start(), calls=%async_computation.4 | async-start | bytes 18874368 | tf_op jit(solution)/shard_map/reduce_scatter | solution.py:31
  162.5 368.9 %reduce-scatter.6.cloned.1.call-start = ((), (), s32[]{:S(2)}) async-start(), calls=%async_computation.6 | async-start | bytes 18874368 | tf_op jit(solution)/shard_map/reduce_scatter | solution.py:31
  252.5 42.5 %copy-start.1 = (f32[4096]{0:T(1024)S(1)}, f32[4096]{0:T(1024)}, u32[]{:S(2)}) copy-start(f32[4096]{0:T(1024)} %param.11) | copy-start | bytes 49156
  252.5 42.5 %copy-start.2 = (s32[4096]{0:T(1024)S(1)}, s32[4096]{0:T(1024)}, u32[]{:S(2)}) copy-start(s32[4096]{0:T(1024)} %param.13) | copy-start | bytes 49156
  252.5 42.5 %copy-start.3 = (s32[4096]{0:T(1024)S(1)}, s32[4096]{0:T(1024)}, u32[]{:S(2)}) copy-start(s32[4096]{0:T(1024)} %param.12) | copy-start | bytes 49156
  252.5 278.8 %copy-start = (f32[4096]{0:T(1024)S(1)}, f32[4096]{0:T(1024)}, u32[]{:S(2)}) copy-start(f32[4096]{0:T(1024)} %param.10) | copy-start | bytes 49156
  252.5 329.3 %reduce-scatter.8.cloned.1.call-start = ((), (), s32[]{:S(2)}) async-start(), calls=%async_computation.7 | async-start | bytes 2621440 | tf_op jit(solution)/shard_map/reduce_scatter | solution.py:40
  531.3 3.6 copy-start.4
Sparse Core Ops, SparseCore 0:
  11.4 90.2 all-gather.2
  103.6 87.5 all-gather.4
  193.6 168.8 reduce-scatter.3
  364.7 166.6 reduce-scatter.5
  548.2 33.5 reduce-scatter.7
